TPU v7x, 32 devices: a whole 2x2x4 slice. The times are simulated.
32 devices in a mesh: group: 4 (over y, x), member: 8 (over z, core).
Axes of the slice: x: 2, y: 2, z: 4, core: 2. Of those that a mesh axis runs over, the one named last changes fastest.
Arguments:
- level_set: bfloat16 [256, 128, 2048], P(('group', 'member')), may hold values from -6 to 6
- ray_length: int32 [128, 2048], replicated, may hold values from 64 to 256
- member_flip: int32 [4], P('group'), may hold values from 0 to 7
- group_flip: int32 [1], replicated, may hold values from 0 to 31
Outputs:
- final_image: float32 [5, 262144], P(None, ('group', 'member'))
Inputs may be any that keep to these rules, and one draw needn't show every extreme that they name: `ray_length`: each entry is a ray's length in depth samples. `member_flip`: bit patterns of the viewing direction along the splits inside a block. `group_flip`: bit pattern of the viewing direction along all splits.
All inputs are finite; a program needn't handle non-finite values.
Results may differ from a plain program's by a relative error of at most 0.0003.
Values sent between devices are 32-bit elements; how exact they have to be, the bound alone decides.
A program may use at most 128 MiB of HBM per device.

v0:
```python
import functools
import math

import jax
import jax.numpy as jnp
from jax import lax
from jax.experimental import pallas as pl
from jax.experimental.pallas import tpu as pltpu
from jax.sharding import PartitionSpec as P

MESH = pl.DeviceIdType.MESH
LANES = 128
PAD = 8


def flip_bit(index, bit):
    own = (index // (1 << bit)) % 2
    return index + (1 - 2 * own) * (1 << bit), own


def kernel(cfg, level_ref, ray_ref, mflip_ref, gflip_ref, out_ref,
           level_here, ray_here, fetch_sem, ray_sem, lev, part, *rest):
    groups, members, bits, slices, rows, cols, subs, block = cfg
    depths = slices * members * groups
    arrive, from_group = rest[:bits], rest[bits]
    send_sem, recv_sem, gsend_sem, grecv_sem = rest[bits + 1:]
    chunks = groups * subs
    chunk_rows = rows // groups
    chunk_cols = cols // subs
    tiles_wide = chunk_cols // LANES
    width = min(512, chunk_cols)

    group_id = lax.axis_index("group")
    member_id = lax.axis_index("member")
    whole_flip = gflip_ref[0]
    member_mask = jnp.bitwise_xor(mflip_ref[0], whole_flip % members)
    group_mask = whole_flip // members
    member_rank = jnp.bitwise_xor(member_id, member_mask)
    group_rank = jnp.bitwise_xor(group_id, group_mask)
    first = (group_rank * members + member_rank) * slices

    barrier = pltpu.get_barrier_semaphore()
    for bit in range(bits):
        partner, _ = flip_bit(member_id, bit)
        pl.semaphore_signal(barrier, inc=1, device_id=(group_id, partner), device_id_type=MESH)
    for step in range(groups - 1):
        other = (group_id + 1 + step) % groups
        pl.semaphore_signal(barrier, inc=1, device_id=(other, member_id), device_id_type=MESH)

    strips = rows // 16
    start_row = ((group_id + 1) % groups) * chunk_rows
    first_strip = (start_row + chunk_rows % 16) // 16 + strips - 1
    early = min(chunk_rows // 16 + 2, strips)

    def strip_row(p):
        return pl.multiple_of(((first_strip + p) % strips) * 16, 16)

    def fetch(p):
        at = pl.ds(strip_row(p), 16)
        return pltpu.make_async_copy(level_ref.at[:, at, :], level_here.at[:, at, :], fetch_sem.at[p])

    rays = pltpu.make_async_copy(ray_ref, ray_here, ray_sem)
    for p in range(early):
        fetch(p).start()
    rays.start()
    for p in range(early, strips):
        fetch(p).start()

    def unpack(p):
        fetch(p).wait()
        r = strip_row(p)
        for k in range(slices):
            value = level_here[k, pl.ds(r, 16), :].astype(jnp.float32)
            at = pl.ds(pl.multiple_of(r + PAD, 8), 16)
            lev[k, at, LANES:LANES + cols] = value
            lev[k, at, 0:LANES] = jnp.broadcast_to(value[:, 0:1], (16, LANES))
            lev[k, at, LANES + cols:] = jnp.broadcast_to(value[:, cols - 1:cols], (16, LANES))

        @pl.when(r == 0)
        def _():
            for k in range(slices):
                lev[k, 0:PAD, :] = jnp.broadcast_to(
                    lev[k, PAD:PAD + 1, :], (PAD, cols + 2 * LANES))

        @pl.when(r == rows - 16)
        def _():
            for k in range(slices):
                lev[k, PAD + rows:, :] = jnp.broadcast_to(
                    lev[k, PAD + rows - 1:PAD + rows, :], (PAD, cols + 2 * LANES))

    period = slices * members
    base_phase = (2.0 * math.pi / period) * (first % period).astype(jnp.float32)
    band = []
    for c in range(3):
        angle = jnp.full((8, LANES), base_phase + 2.0 * math.pi / 3.0 * c, jnp.float32)
        band.append((0.5 * jnp.cos(angle), 0.5 * jnp.sin(angle)))
    first_real = first.astype(jnp.float32)

    def march(t):
        target = (group_id + 1 + t // subs) % groups
        sub = t % subs
        flat = part.at[t].reshape(5, members * block, LANES)

        @pl.loop(0, (chunk_rows // 8) * (chunk_cols // width))
        def _(i):
            local = (i // (chunk_cols // width)) * 8
            local_col = (i % (chunk_cols // width)) * width
            r0 = pl.multiple_of(target * chunk_rows + local, 8)
            c0 = pl.multiple_of(sub * chunk_cols + local_col, LANES)
            left_samples = ray_here[pl.ds(r0, 8), pl.ds(c0, width)] - first
            through = jnp.ones((8, width), jnp.float32)
            plain = jnp.zeros((8, width), jnp.float32)
            even = odd = distance = plain
            for k in range(slices):
                wide = lev[k, pl.ds(pl.multiple_of(r0 + PAD, 8), 8), pl.ds(c0, width + 2 * LANES)]
                total = width + 2 * LANES
                left = pltpu.roll(wide, 1, 1)[:, LANES:LANES + width]
                right = pltpu.roll(wide, total - 1, 1)[:, LANES:LANES + width]
                phi = wide[:, LANES:LANES + width]
                tall = lev[k, pl.ds(r0, 24), pl.ds(pl.multiple_of(c0 + LANES, LANES), width)]
                across = right - left
                downward = tall[9:17] - tall[7:15]
                facing = (0.48 * across + 0.6 * downward + 1.28) * lax.rsqrt(
                    across * across + downward * downward + 4.0)
                shading = 0.25 + 0.75 * jnp.maximum(facing, 0.0)
                opacity = jnp.exp2(phi * phi * (-4.0 / math.log(2.0)) + math.log2(9.0 / depths))
                opacity = jnp.where(left_samples > k, opacity, 0.0)
                weight = through * opacity
                through = through - weight
                distance = distance + weight * ((first_real + (k + 0.5)) / depths)
                shaded = weight * shading
                plain = plain + shaded
                even = even + shaded * math.cos(2.0 * math.pi * k / period)
                if k:
                    odd = odd + shaded * math.sin(2.0 * math.pi * k / period)
            for j in range(width // LANES):
                cut = slice(j * LANES, (j + 1) * LANES)
                at = pl.ds(local * tiles_wide + local_col // LANES + j, 8, stride=tiles_wide)
                for c in range(3):
                    flat[c, at, :] = (0.5 * plain[:, cut] + band[c][0] * even[:, cut]
                                      - band[c][1] * odd[:, cut])
                flat[3, at, :] = distance[:, cut]
                flat[4, at, :] = through[:, cut]

    def half(source, t, own):
        return source.at[t, :, :, own]

    def swap(bit, t):
        partner, own = flip_bit(member_id, bit)
        source = part if bit == 0 else arrive[bit - 1]
        return pltpu.make_async_remote_copy(
            src_ref=half(source, t, 1 - own), dst_ref=landing(bit, t),
            send_sem=send_sem.at[bit, t], recv_sem=recv_sem.at[bit, t],
            device_id=(group_id, partner), device_id_type=MESH)

    def landing(bit, t):
        held = arrive[bit].at[t]
        if bit < bits - 1:
            held = held.reshape(5, members >> (bit + 1), block, LANES)
        return held

    def hand_over(t):
        target = (group_id + 1 + t // subs) % groups
        return pltpu.make_async_remote_copy(
            src_ref=arrive[bits - 1].at[t], dst_ref=from_group.at[t],
            send_sem=gsend_sem.at[t], recv_sem=grecv_sem.at[t],
            device_id=(target, member_id), device_id_type=MESH)

    def blend(bit, t):
        _, own = flip_bit(member_id, bit)
        swap(bit, t).wait_recv()
        source = part if bit == 0 else arrive[bit - 1]
        mine_front = jnp.bitwise_and(jnp.right_shift(member_rank, bit), 1) == 0
        count = members >> (bit + 1)
        target = landing(bit, t)

        @pl.loop(0, count)
        def _(z):
            def kept(c):
                return source[t, c, z, own]

            def place(c):
                return (c, z) if bit < bits - 1 else (c, 0)
            mine, theirs = kept(4), target[place(4)]
            keep_scale = jnp.where(mine_front, 1.0, theirs)
            come_scale = jnp.where(mine_front, mine, 1.0)
            for c in range(4):
                target[place(c)] = keep_scale * kept(c) + come_scale * target[place(c)]
            target[place(4)] = mine * theirs

    pl.loop(0, early)(unpack)
    rays.wait()
    march(0)
    pl.semaphore_wait(barrier, bits + groups - 1)

    delay = [0] + [3 * b - 1 for b in range(1, bits)]

    @pl.loop(0, chunks + delay[-1])
    def _(t):
        @pl.when(t < chunks)
        def _():
            swap(0, t).start()

        @pl.when(t == subs - 1)
        def _():
            pl.loop(early, strips)(unpack)

        @pl.when(t < chunks - 1)
        def _():
            march(t + 1)
        for bit in range(bits):
            now = t - delay[bit]

            @pl.when((now >= 0) & (now < chunks))
            def _():
                blend(bit, now)
                if bit < bits - 1:
                    swap(bit + 1, now).start()
                else:
                    @pl.when(now < chunks - subs)
                    def _():
                        hand_over(now).start()

    @pl.loop(0, chunks - subs)
    def _(t):
        hand_over(t).wait_recv()

    senders = [(group_id + 2 * groups - 1 - i) % groups for i in range(groups)]
    ranks = [jnp.bitwise_xor(s, group_mask) for s in senders]
    for s in range(subs):
        images = [from_group.at[i * subs + s] for i in range(groups - 1)]
        images.append(arrive[bits - 1].at[(groups - 1) * subs + s, :, 0])

        def piece(i, c):
            if i < groups - 1:
                return images[i][c, 0]
            return images[i][c]
        clear = [piece(i, 4) for i in range(groups)]
        total = [None] * 4
        for i in range(groups):
            ahead = None
            for h in range(groups):
                if h != i:
                    term = jnp.where(ranks[h] < ranks[i], clear[h], 1.0)
                    ahead = term if ahead is None else ahead * term
            for c in range(4):
                term = ahead * piece(i, c)
                total[c] = term if total[c] is None else total[c] + term
        for c in range(4):
            out_ref[c, s] = total[c]
        out_ref[4, s] = 1.0 - functools.reduce(lambda a, b: a * b, clear)

    @pl.loop(0, chunks)
    def _(t):
        for bit in range(bits):
            swap(bit, t).wait_send()

    @pl.loop(0, chunks - subs)
    def _(t):
        hand_over(t).wait_send()


def body(groups, members, level_set, ray_length, member_flip, group_flip):
    slices, rows, cols = level_set.shape
    bits = members.bit_length() - 1
    pixels = rows * cols // (groups * members)
    whole_rows = pixels % cols == 0
    subs = 1
    while whole_rows and subs < 4 and pixels % (2 * subs * 8 * LANES) == 0:
        subs *= 2
    block = pixels // LANES // subs
    chunks = groups * subs
    cfg = (groups, members, bits, slices, rows, cols, subs, block)
    arrive = []
    for bit in range(bits):
        count = members >> (bit + 1)
        shape = (count // 2, 2) if bit < bits - 1 else (1,)
        arrive.append(pltpu.VMEM((chunks, 5) + shape + (block, LANES), jnp.float32))
    vmem = pl.BlockSpec(memory_space=pltpu.VMEM)
    anywhere = pl.BlockSpec(memory_space=pl.ANY)
    smem = pl.BlockSpec(memory_space=pltpu.SMEM)
    image = pl.pallas_call(
        functools.partial(kernel, cfg),
        out_shape=jax.ShapeDtypeStruct((5, subs, block, LANES), jnp.float32),
        in_specs=[anywhere, anywhere, smem, smem],
        out_specs=vmem,
        scratch_shapes=[
            pltpu.VMEM((slices, rows, cols), level_set.dtype),
            pltpu.VMEM((rows, cols), ray_length.dtype),
            pltpu.SemaphoreType.DMA((rows // 16,)),
            pltpu.SemaphoreType.DMA,
            pltpu.VMEM((slices, rows + 2 * PAD, cols + 2 * LANES), jnp.float32),
            pltpu.VMEM((chunks, 5, members // 2, 2, block, LANES), jnp.float32),
            *arrive,
            pltpu.VMEM((chunks - subs, 5, 1, block, LANES), jnp.float32),
            pltpu.SemaphoreType.DMA((bits, chunks)),
            pltpu.SemaphoreType.DMA((bits, chunks)),
            pltpu.SemaphoreType.DMA((chunks - subs,)),
            pltpu.SemaphoreType.DMA((chunks - subs,)),
        ],
        compiler_params=pltpu.CompilerParams(
            collective_id=0, has_side_effects=True, vmem_limit_bytes=60 * 1024 * 1024),
        cost_estimate=pl.CostEstimate(
            flops=40 * slices * rows * cols, bytes_accessed=level_set.size * 2,
            transcendentals=2 * slices * rows * cols),
    )(level_set, ray_length, member_flip, group_flip)
    if subs > 1:
        image = image.reshape(5, subs, pixels // cols, cols // subs).transpose(0, 2, 1, 3)
    return image.reshape(5, pixels)


def solution(mesh):
    in_specs = (P(("group", "member"), None, None), P(), P("group"), P())
    out_specs = P(None, ("group", "member"))
    run = functools.partial(body, mesh.shape["group"], mesh.shape["member"])
    return jax.shard_map(run, mesh=mesh, in_specs=in_specs, out_specs=out_specs, check_vma=False)
```

profile of v0, /device:TPU:0, one launch (start us, length us, event | category | flops | bytes accessed | tf_op | source)
XLA Modules:
  0.0 58.0 jit_solution(9639264590150973508)
XLA Ops:
  1.3 54.8 %shard_map.46 = f32[5,4,16,128]{3,2,1,0:T(8,128)} custom-call(bf16[8,128,2048]{2,1,0:T(8,128)(2,1)} %level_ref.1, s32[128,2048]{1,0:T(8,128)} %ray_ref.1, s32[1]{0:T(128)S(6)} %copy.6.mflip_ref, s32[1]{0:T(128)S(6)} %copy.7.gflip_ref), custom_call_target="tpu_custom_call" | custom-call | flops 83886080 | bytes 4194304 | tf_op jit(solution)/shard_map/pallas_call | solution.py:282
  56.1 1.0 %reshape.6 = f32[5,4,4,512]{3,2,1,0:T(4,128)S(1)} reshape(f32[5,4,16,128]{3,2,1,0:T(8,128)} %shard_map.46) | data formatting | bytes 327680 | tf_op jit(solution)/shard_map/reshape | solution.py:308
  57.1 0.1 copy.5
  57.2 0.8 %reshape.7 = f32[5,8192]{1,0:T(8,128)} reshape(f32[5,4,4,512]{3,2,1,0:T(4,128)S(1)} %copy.5) | data formatting | bytes 327680 | tf_op jit(solution)/shard_map/reshape | solution.py:309
where the time goes:
time: 58.1 us; the launch traced here: 58 us
  Pallas kernels  54.8 us (94%)
  local copies, waits for them, and re-layouts  1.85 us (3%)
  between operations  1.32 us (2%)
    pallas_call x1, Pallas kernels, body(): pl.pallas_call(functools.partial(kernel, cfg), out_shape=jax.ShapeDtypeSt...  54.8 us

commit v1 on v0

--- a/solution.py
+++ b/solution.py
@@ -22,8 +22,8 @@
            level_here, ray_here, fetch_sem, ray_sem, lev, part, *rest):
     groups, members, bits, slices, rows, cols, subs, block = cfg
     depths = slices * members * groups
-    arrive, from_group = rest[:bits], rest[bits]
-    send_sem, recv_sem, gsend_sem, grecv_sem = rest[bits + 1:]
+    arrive, clear_in, sums = rest[0], rest[1:bits], rest[bits:2 * bits]
+    from_group, send_sem, recv_sem, sum_send, sum_recv, gsend_sem, grecv_sem = rest[2 * bits:]
     chunks = groups * subs
     chunk_rows = rows // groups
     chunk_cols = cols // subs
@@ -97,8 +97,8 @@
     first_real = first.astype(jnp.float32)
 
     def march(t):
-        target = (group_id + 1 + t // subs) % groups
-        sub = t % subs
+        target = (group_id + 1 + t % groups) % groups
+        sub = t // groups
         flat = part.at[t].reshape(5, members * block, LANES)
 
         @pl.loop(0, (chunk_rows // 8) * (chunk_cols // width))
@@ -142,58 +142,132 @@
                 flat[3, at, :] = distance[:, cut]
                 flat[4, at, :] = through[:, cut]
 
-    def half(source, t, own):
-        return source.at[t, :, :, own]
+    def partner_of(bit):
+        partner, own = flip_bit(member_id, bit)
+        mine_front = jnp.bitwise_and(jnp.right_shift(member_rank, bit), 1) == 0
+        return (group_id, partner), own, mine_front
 
     def swap(bit, t):
-        partner, own = flip_bit(member_id, bit)
-        source = part if bit == 0 else arrive[bit - 1]
+        partner, own, _ = partner_of(bit)
+        if bit == 0:
+            source, target = part.at[t, :, :, 1 - own], arrive.at[t]
+        else:
+            source = arrive.at[t, 4] if bit == 1 else clear_in[bit - 2].at[t]
+            target = clear_in[bit - 1].at[t]
         return pltpu.make_async_remote_copy(
-            src_ref=half(source, t, 1 - own), dst_ref=landing(bit, t),
+            src_ref=source, dst_ref=target,
             send_sem=send_sem.at[bit, t], recv_sem=recv_sem.at[bit, t],
-            device_id=(group_id, partner), device_id_type=MESH)
-
-    def landing(bit, t):
-        held = arrive[bit].at[t]
-        if bit < bits - 1:
-            held = held.reshape(5, members >> (bit + 1), block, LANES)
-        return held
+            device_id=partner, device_id_type=MESH)
+
+    def slot(t):
+        return (t // groups) * (groups - 1) + t % groups
 
     def hand_over(t):
-        target = (group_id + 1 + t // subs) % groups
+        target = (group_id + 1 + t % groups) % groups
         return pltpu.make_async_remote_copy(
-            src_ref=arrive[bits - 1].at[t], dst_ref=from_group.at[t],
-            send_sem=gsend_sem.at[t], recv_sem=grecv_sem.at[t],
+            src_ref=arrive.at[t], dst_ref=from_group.at[slot(t)],
+            send_sem=gsend_sem.at[slot(t)], recv_sem=grecv_sem.at[slot(t)],
             device_id=(target, member_id), device_id_type=MESH)
 
-    def blend(bit, t):
-        _, own = flip_bit(member_id, bit)
-        swap(bit, t).wait_recv()
-        source = part if bit == 0 else arrive[bit - 1]
-        mine_front = jnp.bitwise_and(jnp.right_shift(member_rank, bit), 1) == 0
-        count = members >> (bit + 1)
-        target = landing(bit, t)
-
-        @pl.loop(0, count)
+    def blend_cores(t):
+        _, own, mine_front = partner_of(0)
+        swap(0, t).wait_recv()
+
+        @pl.loop(0, members // 2)
         def _(z):
-            def kept(c):
-                return source[t, c, z, own]
-
-            def place(c):
-                return (c, z) if bit < bits - 1 else (c, 0)
-            mine, theirs = kept(4), target[place(4)]
+            mine, theirs = part[t, 4, z, own], arrive[t, 4, z]
             keep_scale = jnp.where(mine_front, 1.0, theirs)
             come_scale = jnp.where(mine_front, mine, 1.0)
             for c in range(4):
-                target[place(c)] = keep_scale * kept(c) + come_scale * target[place(c)]
-            target[place(4)] = mine * theirs
+                arrive[t, c, z] = keep_scale * part[t, c, z, own] + come_scale * arrive[t, c, z]
+            arrive[t, 4, z] = mine * theirs
+
+    def attenuate(bit, t):
+        _, _, mine_front = partner_of(bit)
+        swap(bit, t).wait_recv()
+        if bit == bits - 1:
+            swap(1, t).wait_send()
+
+        @pl.loop(0, members // 2)
+        def _(z):
+            mine = arrive[t, 4, z] if bit == 1 else clear_in[bit - 2][t, z]
+            theirs = clear_in[bit - 1][t, z]
+            scale = jnp.where(mine_front, 1.0, theirs)
+            for c in range(4):
+                arrive[t, c, z] = scale * arrive[t, c, z]
+            if bit < bits - 1:
+                clear_in[bit - 1][t, z] = mine * theirs
+            else:
+                arrive[t, 4, z] = mine * theirs
+
+    def summed(level, s):
+        return sums[level].at[s].reshape(4, members >> (level + 1), block, LANES)
+
+    def sum_swap(bit, s):
+        partner, own, _ = partner_of(bit)
+        return pltpu.make_async_remote_copy(
+            src_ref=sums[bit - 1].at[s, :, :, 1 - own], dst_ref=summed(bit, s),
+            send_sem=sum_send.at[bit, s], recv_sem=sum_recv.at[bit, s],
+            device_id=partner, device_id_type=MESH)
+
+    def put(c, s, value):
+        for q in range(block):
+            at = (q // tiles_wide) * cols + (q % tiles_wide) * LANES
+            at = pl.ds(pl.multiple_of(s * chunk_cols + at, LANES), LANES)
+            out_ref[c:c + 1, at] = value[q:q + 1, :]
+
+    senders = [(group_id + 2 * groups - 1 - i) % groups for i in range(groups)]
+    ranks = [jnp.bitwise_xor(s, group_mask) for s in senders]
+
+    def merge_groups(s):
+        for i in range(groups - 1):
+            hand_over(s * groups + i).wait_recv()
+
+        def piece(i, c, z):
+            if i < groups - 1:
+                return from_group[s * (groups - 1) + i, c, z]
+            return arrive[s * groups + i, c, z]
+        target = summed(0, s)
+
+        @pl.loop(0, members // 2)
+        def _(z):
+            clear = [piece(i, 4, z) for i in range(groups)]
+            total = [None] * 4
+            for i in range(groups):
+                ahead = None
+                for h in range(groups):
+                    if h != i:
+                        term = jnp.where(ranks[h] < ranks[i], clear[h], 1.0)
+                        ahead = term if ahead is None else ahead * term
+                for c in range(4):
+                    term = ahead * piece(i, c, z)
+                    total[c] = term if total[c] is None else total[c] + term
+            for c in range(4):
+                target[c, z] = total[c]
+
+            @pl.when(z == member_id // 2)
+            def _():
+                put(4, s, 1.0 - functools.reduce(lambda a, b: a * b, clear))
+
+    def add_up(bit, s):
+        _, own, _ = partner_of(bit)
+        sum_swap(bit, s).wait_recv()
+        target = summed(bit, s)
+        if bit == bits - 1:
+            for c in range(4):
+                put(c, s, sums[bit - 1][s, c, 0, own] + target[c, 0])
+        else:
+            @pl.loop(0, members >> (bit + 1))
+            def _(z):
+                for c in range(4):
+                    target[c, z] = target[c, z] + sums[bit - 1][s, c, z, own]
 
     pl.loop(0, early)(unpack)
     rays.wait()
     march(0)
     pl.semaphore_wait(barrier, bits + groups - 1)
 
-    delay = [0] + [3 * b - 1 for b in range(1, bits)]
+    delay = [2 * bit for bit in range(2 * bits)]
 
     @pl.loop(0, chunks + delay[-1])
     def _(t):
@@ -201,7 +275,7 @@
         def _():
             swap(0, t).start()
 
-        @pl.when(t == subs - 1)
+        @pl.when(t == 0)
         def _():
             pl.loop(early, strips)(unpack)
 
@@ -213,51 +287,44 @@
 
             @pl.when((now >= 0) & (now < chunks))
             def _():
-                blend(bit, now)
+                if bit == 0:
+                    blend_cores(now)
+                else:
+                    attenuate(bit, now)
                 if bit < bits - 1:
                     swap(bit + 1, now).start()
                 else:
-                    @pl.when(now < chunks - subs)
+                    @pl.when(now % groups != groups - 1)
                     def _():
                         hand_over(now).start()
 
-    @pl.loop(0, chunks - subs)
-    def _(t):
-        hand_over(t).wait_recv()
-
-    senders = [(group_id + 2 * groups - 1 - i) % groups for i in range(groups)]
-    ranks = [jnp.bitwise_xor(s, group_mask) for s in senders]
-    for s in range(subs):
-        images = [from_group.at[i * subs + s] for i in range(groups - 1)]
-        images.append(arrive[bits - 1].at[(groups - 1) * subs + s, :, 0])
-
-        def piece(i, c):
-            if i < groups - 1:
-                return images[i][c, 0]
-            return images[i][c]
-        clear = [piece(i, 4) for i in range(groups)]
-        total = [None] * 4
-        for i in range(groups):
-            ahead = None
-            for h in range(groups):
-                if h != i:
-                    term = jnp.where(ranks[h] < ranks[i], clear[h], 1.0)
-                    ahead = term if ahead is None else ahead * term
-            for c in range(4):
-                term = ahead * piece(i, c)
-                total[c] = term if total[c] is None else total[c] + term
-        for c in range(4):
-            out_ref[c, s] = total[c]
-        out_ref[4, s] = 1.0 - functools.reduce(lambda a, b: a * b, clear)
+        for bit in range(bits):
+            now = t - delay[bits + bit]
+
+            @pl.when((now >= 0) & (now < chunks) & (now % groups == groups - 1))
+            def _():
+                cut = now // groups
+                if bit == 0:
+                    merge_groups(cut)
+                else:
+                    add_up(bit, cut)
+                if bit < bits - 1:
+                    sum_swap(bit + 1, cut).start()
 
     @pl.loop(0, chunks)
     def _(t):
         for bit in range(bits):
-            swap(bit, t).wait_send()
-
-    @pl.loop(0, chunks - subs)
-    def _(t):
-        hand_over(t).wait_send()
+            if bit != 1:
+                swap(bit, t).wait_send()
+
+        @pl.when(t % groups != groups - 1)
+        def _():
+            hand_over(t).wait_send()
+
+    @pl.loop(0, subs)
+    def _(s):
+        for bit in range(1, bits):
+            sum_swap(bit, s).wait_send()
 
 
 def body(groups, members, level_set, ray_length, member_flip, group_flip):
@@ -271,17 +338,18 @@
     block = pixels // LANES // subs
     chunks = groups * subs
     cfg = (groups, members, bits, slices, rows, cols, subs, block)
-    arrive = []
+    half = members // 2
+    sums = []
     for bit in range(bits):
         count = members >> (bit + 1)
         shape = (count // 2, 2) if bit < bits - 1 else (1,)
-        arrive.append(pltpu.VMEM((chunks, 5) + shape + (block, LANES), jnp.float32))
+        sums.append(pltpu.VMEM((subs, 4) + shape + (block, LANES), jnp.float32))
     vmem = pl.BlockSpec(memory_space=pltpu.VMEM)
     anywhere = pl.BlockSpec(memory_space=pl.ANY)
     smem = pl.BlockSpec(memory_space=pltpu.SMEM)
-    image = pl.pallas_call(
+    return pl.pallas_call(
         functools.partial(kernel, cfg),
-        out_shape=jax.ShapeDtypeStruct((5, subs, block, LANES), jnp.float32),
+        out_shape=jax.ShapeDtypeStruct((5, pixels), jnp.float32),
         in_specs=[anywhere, anywhere, smem, smem],
         out_specs=vmem,
         scratch_shapes=[
@@ -291,12 +359,13 @@
             pltpu.SemaphoreType.DMA,
             pltpu.VMEM((slices, rows + 2 * PAD, cols + 2 * LANES), jnp.float32),
             pltpu.VMEM((chunks, 5, members // 2, 2, block, LANES), jnp.float32),
-            *arrive,
-            pltpu.VMEM((chunks - subs, 5, 1, block, LANES), jnp.float32),
-            pltpu.SemaphoreType.DMA((bits, chunks)),
-            pltpu.SemaphoreType.DMA((bits, chunks)),
-            pltpu.SemaphoreType.DMA((chunks - subs,)),
-            pltpu.SemaphoreType.DMA((chunks - subs,)),
+            pltpu.VMEM((chunks, 5, half, block, LANES), jnp.float32),
+            *[pltpu.VMEM((chunks, half, block, LANES), jnp.float32)] * (bits - 1),
+            *sums,
+            pltpu.VMEM((chunks - subs, 5, half, block, LANES), jnp.float32),
+            *[pltpu.SemaphoreType.DMA((bits, chunks))] * 2,
+            *[pltpu.SemaphoreType.DMA((bits, subs))] * 2,
+            *[pltpu.SemaphoreType.DMA((chunks - subs,))] * 2,
         ],
         compiler_params=pltpu.CompilerParams(
             collective_id=0, has_side_effects=True, vmem_limit_bytes=60 * 1024 * 1024),
@@ -304,9 +373,6 @@
             flops=40 * slices * rows * cols, bytes_accessed=level_set.size * 2,
             transcendentals=2 * slices * rows * cols),
     )(level_set, ray_length, member_flip, group_flip)
-    if subs > 1:
-        image = image.reshape(5, subs, pixels // cols, cols // subs).transpose(0, 2, 1, 3)
-    return image.reshape(5, pixels)
 
 
 def solution(mesh):

time: 58.1 us -> 62 us (1.067)
  Pallas kernels: 54.8 us -> 58.8 us
    pallas_call x1, Pallas kernels: 54.8 us -> 58.8 us  [body(): pl.pallas_call(functools.partial(kernel, cfg), out_shape=jax.ShapeDtypeSt...]
    reshape x2 -> x0, local copies, waits for them, and re-layouts: 1.79 us -> none  [the longest x1 0.97 us: body(): image.reshape(5, subs, pixels // cols, cols // subs).transpose(0, 2, 1, 3)]
    unnamed x0 -> x1, local copies, waits for them, and re-layouts: none -> 1.67 us
where the time goes in v1:
time: 62 us; the launch traced here: 61.8 us
  Pallas kernels  58.8 us (95%)
  local copies, waits for them, and re-layouts  1.67 us (3%)
  between operations  1.3 us (2%)
    pallas_call x1, Pallas kernels, body(): pl.pallas_call(functools.partial(kernel, cfg), out_shape=jax.ShapeDtypeSt...  58.8 us
    unnamed x1, local copies, waits for them, and re-layouts  1.67 us

profile of v1, /device:TPU:0, one launch (start us, length us, event | category | flops | bytes accessed | tf_op | source)
XLA Modules:
  0.0 61.8 jit_solution(13228859877799847568)
XLA Ops:
  1.3 58.8 %shard_map.46 = f32[5,8192]{1,0:T(8,128)} custom-call(bf16[8,128,2048]{2,1,0:T(8,128)(2,1)} %level_ref.1, s32[128,2048]{1,0:T(8,128)} %ray_ref.1, s32[1]{0:T(128)S(6)} %copy.6.mflip_ref, s32[1]{0:T(128)S(6)} %copy.7.gflip_ref), custom_call_target="tpu_custom_call" | custom-call | flops 83886080 | bytes 4194304 | tf_op jit(solution)/shard_map/pallas_call | solution.py:350
  60.1 1.7 %copy.8 = f32[5,8192]{1,0:T(8,128)} copy(f32[5,8192]{1,0:T(8,128)} %shard_map.46) | data formatting | bytes 327680

commit v2 on v1

--- a/solution.py
+++ b/solution.py
@@ -10,7 +10,7 @@
 
 MESH = pl.DeviceIdType.MESH
 LANES = 128
-PAD = 8
+PAD = 16
 
 
 def flip_bit(index, bit):
@@ -19,7 +19,7 @@
 
 
 def kernel(cfg, level_ref, ray_ref, mflip_ref, gflip_ref, out_ref,
-           level_here, ray_here, fetch_sem, ray_sem, lev, part, *rest):
+           level_here, ray_here, fetch_sem, ray_sem, across_held, down_held, part, *rest):
     groups, members, bits, slices, rows, cols, subs, block = cfg
     depths = slices * members * groups
     arrive, clear_in, sums = rest[0], rest[1:bits], rest[bits:2 * bits]
@@ -28,7 +28,6 @@
     chunk_rows = rows // groups
     chunk_cols = cols // subs
     tiles_wide = chunk_cols // LANES
-    width = min(512, chunk_cols)
 
     group_id = lax.axis_index("group")
     member_id = lax.axis_index("member")
@@ -49,15 +48,16 @@
 
     strips = rows // 16
     start_row = ((group_id + 1) % groups) * chunk_rows
-    first_strip = (start_row + chunk_rows % 16) // 16 + strips - 1
-    early = min(chunk_rows // 16 + 2, strips)
+    first_strip = start_row // 16 + strips - 1
+    early = min(max(chunk_rows // 16, 1) + 2, strips)
 
     def strip_row(p):
         return pl.multiple_of(((first_strip + p) % strips) * 16, 16)
 
     def fetch(p):
         at = pl.ds(strip_row(p), 16)
-        return pltpu.make_async_copy(level_ref.at[:, at, :], level_here.at[:, at, :], fetch_sem.at[p])
+        return pltpu.make_async_copy(level_ref.at[:, at, :],
+            level_here.at[:, pl.ds(strip_row(p) + PAD, 16), pl.ds(LANES, cols)], fetch_sem.at[p])
 
     rays = pltpu.make_async_copy(ray_ref, ray_here, ray_sem)
     for p in range(early):
@@ -69,30 +69,44 @@
     def unpack(p):
         fetch(p).wait()
         r = strip_row(p)
+        at = pl.ds(pl.multiple_of(r + PAD, 16), 16)
         for k in range(slices):
-            value = level_here[k, pl.ds(r, 16), :].astype(jnp.float32)
-            at = pl.ds(pl.multiple_of(r + PAD, 8), 16)
-            lev[k, at, LANES:LANES + cols] = value
-            lev[k, at, 0:LANES] = jnp.broadcast_to(value[:, 0:1], (16, LANES))
-            lev[k, at, LANES + cols:] = jnp.broadcast_to(value[:, cols - 1:cols], (16, LANES))
+            start = level_here[k, at, LANES:2 * LANES].astype(jnp.float32)[:, 0:1]
+            end = level_here[k, at, cols:cols + LANES].astype(jnp.float32)[:, LANES - 1:LANES]
+            level_here[k, at, 0:LANES] = jnp.broadcast_to(start, (16, LANES)).astype(jnp.bfloat16)
+            level_here[k, at, LANES + cols:] = jnp.broadcast_to(end, (16, LANES)).astype(jnp.bfloat16)
 
         @pl.when(r == 0)
         def _():
             for k in range(slices):
-                lev[k, 0:PAD, :] = jnp.broadcast_to(
-                    lev[k, PAD:PAD + 1, :], (PAD, cols + 2 * LANES))
+                edge = level_here[k, PAD:PAD + 16, :].astype(jnp.float32)[0:1]
+                level_here[k, 0:PAD, :] = jnp.broadcast_to(
+                    edge, (PAD, cols + 2 * LANES)).astype(jnp.bfloat16)
 
         @pl.when(r == rows - 16)
         def _():
             for k in range(slices):
-                lev[k, PAD + rows:, :] = jnp.broadcast_to(
-                    lev[k, PAD + rows - 1:PAD + rows, :], (PAD, cols + 2 * LANES))
+                edge = level_here[k, rows:PAD + rows, :].astype(jnp.float32)[15:16]
+                level_here[k, PAD + rows:, :] = jnp.broadcast_to(
+                    edge, (PAD, cols + 2 * LANES)).astype(jnp.bfloat16)
+
+    def differences(shape, near, far, offset):
+        a = lax.broadcasted_iota(jnp.int32, shape, near)
+        b = lax.broadcasted_iota(jnp.int32, shape, far) - offset
+        up = jnp.where(b == a + 1, 1.0, 0.0)
+        return (up - jnp.where(b == a - 1, 1.0, 0.0)).astype(jnp.bfloat16)
+
+    span = min(256, chunk_cols)
+    lane_matrix = differences((span + 2 * LANES, span), 1, 0, LANES)
+    tall = max(chunk_rows, 16)
+    high = min(chunk_rows, 16)
+    width = min(4096 // high, chunk_cols)
 
     period = slices * members
     base_phase = (2.0 * math.pi / period) * (first % period).astype(jnp.float32)
     band = []
     for c in range(3):
-        angle = jnp.full((8, LANES), base_phase + 2.0 * math.pi / 3.0 * c, jnp.float32)
+        angle = jnp.full((min(chunk_rows, 16), LANES), base_phase + 2.0 * math.pi / 3.0 * c, jnp.float32)
         band.append((0.5 * jnp.cos(angle), 0.5 * jnp.sin(angle)))
     first_real = first.astype(jnp.float32)
 
@@ -101,25 +115,45 @@
         sub = t // groups
         flat = part.at[t].reshape(5, members * block, LANES)
 
-        @pl.loop(0, (chunk_rows // 8) * (chunk_cols // width))
+        row0 = target * chunk_rows
+        base = pl.multiple_of((row0 // 16) * 16, 16)
+        offset = row0 % 16
+        c_first = pl.multiple_of(sub * chunk_cols, LANES)
+        row_matrix = differences((chunk_rows, tall + 32), 0, 1, PAD + offset)
+
+        def own_rows(value):
+            if chunk_rows % 16 == 0:
+                return value
+            return jnp.where(offset == 0, value[0:8], value[8:16])
+
+        @pl.loop(0, slices)
+        def _(k):
+            for j in range(chunk_cols // span):
+                here = slice(j * span, (j + 1) * span)
+                at = pl.multiple_of(c_first + j * span, LANES)
+                window = level_here[k, pl.ds(base + PAD, tall), pl.ds(at, span + 2 * LANES)]
+                across_held[k, :, here] = own_rows(
+                    jnp.dot(window, lane_matrix, preferred_element_type=jnp.float32))
+                window = level_here[k, pl.ds(base, tall + 32), pl.ds(at + LANES, span)]
+                down_held[k, :, here] = jnp.dot(
+                    row_matrix, window, preferred_element_type=jnp.float32)
+
+        @pl.loop(0, (chunk_rows // high) * (chunk_cols // width))
         def _(i):
-            local = (i // (chunk_cols // width)) * 8
-            local_col = (i % (chunk_cols // width)) * width
-            r0 = pl.multiple_of(target * chunk_rows + local, 8)
-            c0 = pl.multiple_of(sub * chunk_cols + local_col, LANES)
-            left_samples = ray_here[pl.ds(r0, 8), pl.ds(c0, width)] - first
-            through = jnp.ones((8, width), jnp.float32)
-            plain = jnp.zeros((8, width), jnp.float32)
+            local = pl.multiple_of((i // (chunk_cols // width)) * high, high)
+            local_col = pl.multiple_of((i % (chunk_cols // width)) * width, LANES)
+            r0 = pl.multiple_of(row0 + local, 8)
+            c0 = pl.multiple_of(c_first + local_col, LANES)
+            left_samples = ray_here[pl.ds(r0, high), pl.ds(c0, width)] - first
+            through = jnp.ones((high, width), jnp.float32)
+            plain = jnp.zeros((high, width), jnp.float32)
             even = odd = distance = plain
             for k in range(slices):
-                wide = lev[k, pl.ds(pl.multiple_of(r0 + PAD, 8), 8), pl.ds(c0, width + 2 * LANES)]
-                total = width + 2 * LANES
-                left = pltpu.roll(wide, 1, 1)[:, LANES:LANES + width]
-                right = pltpu.roll(wide, total - 1, 1)[:, LANES:LANES + width]
-                phi = wide[:, LANES:LANES + width]
-                tall = lev[k, pl.ds(r0, 24), pl.ds(pl.multiple_of(c0 + LANES, LANES), width)]
-                across = right - left
-                downward = tall[9:17] - tall[7:15]
+                phi = own_rows(level_here[
+                    k, pl.ds(pl.multiple_of(base + PAD + local, 16), 16),
+                    pl.ds(c0 + LANES, width)].astype(jnp.float32))
+                across = across_held[k, pl.ds(local, high), pl.ds(local_col, width)]
+                downward = down_held[k, pl.ds(local, high), pl.ds(local_col, width)]
                 facing = (0.48 * across + 0.6 * downward + 1.28) * lax.rsqrt(
                     across * across + downward * downward + 4.0)
                 shading = 0.25 + 0.75 * jnp.maximum(facing, 0.0)
@@ -135,7 +169,7 @@
                     odd = odd + shaded * math.sin(2.0 * math.pi * k / period)
             for j in range(width // LANES):
                 cut = slice(j * LANES, (j + 1) * LANES)
-                at = pl.ds(local * tiles_wide + local_col // LANES + j, 8, stride=tiles_wide)
+                at = pl.ds(local * tiles_wide + local_col // LANES + j, high, stride=tiles_wide)
                 for c in range(3):
                     flat[c, at, :] = (0.5 * plain[:, cut] + band[c][0] * even[:, cut]
                                       - band[c][1] * odd[:, cut])
@@ -353,11 +387,11 @@
         in_specs=[anywhere, anywhere, smem, smem],
         out_specs=vmem,
         scratch_shapes=[
-            pltpu.VMEM((slices, rows, cols), level_set.dtype),
+            pltpu.VMEM((slices, rows + 2 * PAD, cols + 2 * LANES), level_set.dtype),
             pltpu.VMEM((rows, cols), ray_length.dtype),
             pltpu.SemaphoreType.DMA((rows // 16,)),
             pltpu.SemaphoreType.DMA,
-            pltpu.VMEM((slices, rows + 2 * PAD, cols + 2 * LANES), jnp.float32),
+            *[pltpu.VMEM((slices, rows // groups, cols // subs), jnp.float32)] * 2,
             pltpu.VMEM((chunks, 5, members // 2, 2, block, LANES), jnp.float32),
             pltpu.VMEM((chunks, 5, half, block, LANES), jnp.float32),
             *[pltpu.VMEM((chunks, half, block, LANES), jnp.float32)] * (bits - 1),

time: 62 us -> 69.2 us (1.12)
  Pallas kernels: 58.8 us -> 66.1 us
    pallas_call x1, Pallas kernels: 58.8 us -> 66.1 us  [body(): pl.pallas_call(functools.partial(kernel, cfg), out_shape=jax.ShapeDtypeSt...]
where the time goes in v2:
time: 69.2 us; the launch traced here: 69.1 us
  Pallas kernels  66.1 us (96%)
  local copies, waits for them, and re-layouts  1.67 us (2%)
  between operations  1.3 us (2%)
    pallas_call x1, Pallas kernels, body(): pl.pallas_call(functools.partial(kernel, cfg), out_shape=jax.ShapeDtypeSt...  66.1 us
    unnamed x1, local copies, waits for them, and re-layouts  1.67 us

profile of v2, /device:TPU:0, one launch (start us, length us, event | category | flops | bytes accessed | tf_op | source)
XLA Modules:
  0.0 69.1 jit_solution(2735187722741359850)
XLA Ops:
  1.3 66.1 %shard_map.46 = f32[5,8192]{1,0:T(8,128)} custom-call(bf16[8,128,2048]{2,1,0:T(8,128)(2,1)} %level_ref.1, s32[128,2048]{1,0:T(8,128)} %ray_ref.1, s32[1]{0:T(128)S(6)} %copy.6.mflip_ref, s32[1]{0:T(128)S(6)} %copy.7.gflip_ref), custom_call_target="tpu_custom_call" | custom-call | flops 83886080 | bytes 4194304 | tf_op jit(solution)/shard_map/pallas_call | solution.py:384
  67.4 1.7 %copy.8 = f32[5,8192]{1,0:T(8,128)} copy(f32[5,8192]{1,0:T(8,128)} %shard_map.46) | data formatting | bytes 327680

commit v3 on v2

--- a/solution.py
+++ b/solution.py
@@ -19,7 +19,7 @@
 
 
 def kernel(cfg, level_ref, ray_ref, mflip_ref, gflip_ref, out_ref,
-           level_here, ray_here, fetch_sem, ray_sem, across_held, down_held, part, *rest):
+           level_here, ray_here, fetch_sem, ray_sem, across_held, part, *rest):
     groups, members, bits, slices, rows, cols, subs, block = cfg
     depths = slices * members * groups
     arrive, clear_in, sums = rest[0], rest[1:bits], rest[bits:2 * bits]
@@ -99,14 +99,14 @@
     span = min(256, chunk_cols)
     lane_matrix = differences((span + 2 * LANES, span), 1, 0, LANES)
     tall = max(chunk_rows, 16)
-    high = min(chunk_rows, 16)
-    width = min(4096 // high, chunk_cols)
+    high = chunk_rows
+    width = max(LANES, 4096 // high)
 
     period = slices * members
     base_phase = (2.0 * math.pi / period) * (first % period).astype(jnp.float32)
     band = []
     for c in range(3):
-        angle = jnp.full((min(chunk_rows, 16), LANES), base_phase + 2.0 * math.pi / 3.0 * c, jnp.float32)
+        angle = jnp.full((chunk_rows, LANES), base_phase + 2.0 * math.pi / 3.0 * c, jnp.float32)
         band.append((0.5 * jnp.cos(angle), 0.5 * jnp.sin(angle)))
     first_real = first.astype(jnp.float32)
 
@@ -119,28 +119,23 @@
         base = pl.multiple_of((row0 // 16) * 16, 16)
         offset = row0 % 16
         c_first = pl.multiple_of(sub * chunk_cols, LANES)
-        row_matrix = differences((chunk_rows, tall + 32), 0, 1, PAD + offset)
-
         def own_rows(value):
             if chunk_rows % 16 == 0:
                 return value
             return jnp.where(offset == 0, value[0:8], value[8:16])
 
-        @pl.loop(0, slices)
-        def _(k):
-            for j in range(chunk_cols // span):
-                here = slice(j * span, (j + 1) * span)
-                at = pl.multiple_of(c_first + j * span, LANES)
-                window = level_here[k, pl.ds(base + PAD, tall), pl.ds(at, span + 2 * LANES)]
-                across_held[k, :, here] = own_rows(
-                    jnp.dot(window, lane_matrix, preferred_element_type=jnp.float32))
-                window = level_here[k, pl.ds(base, tall + 32), pl.ds(at + LANES, span)]
-                down_held[k, :, here] = jnp.dot(
-                    row_matrix, window, preferred_element_type=jnp.float32)
+        for j in range(chunk_cols // span):
+            here = slice(j * span, (j + 1) * span)
+            at = pl.multiple_of(c_first + j * span, LANES)
+            window = level_here[:, pl.ds(base + PAD, tall), pl.ds(at, span + 2 * LANES)]
+            across = jnp.dot(window.reshape(slices * tall, span + 2 * LANES), lane_matrix,
+                             preferred_element_type=jnp.float32)
+            for k in range(slices):
+                across_held[k, :, here] = own_rows(across[k * tall:(k + 1) * tall])
 
         @pl.loop(0, (chunk_rows // high) * (chunk_cols // width))
         def _(i):
-            local = pl.multiple_of((i // (chunk_cols // width)) * high, high)
+            local = (i // (chunk_cols // width)) * high
             local_col = pl.multiple_of((i % (chunk_cols // width)) * width, LANES)
             r0 = pl.multiple_of(row0 + local, 8)
             c0 = pl.multiple_of(c_first + local_col, LANES)
@@ -149,11 +144,13 @@
             plain = jnp.zeros((high, width), jnp.float32)
             even = odd = distance = plain
             for k in range(slices):
-                phi = own_rows(level_here[
-                    k, pl.ds(pl.multiple_of(base + PAD + local, 16), 16),
-                    pl.ds(c0 + LANES, width)].astype(jnp.float32))
+                window = level_here[
+                    k, pl.ds(pl.multiple_of(base + local, 16), tall + 32),
+                    pl.ds(c0 + LANES, width)].astype(jnp.float32)
+                phi = own_rows(window[PAD:PAD + tall])
+                downward = own_rows(window[PAD + 1:PAD + 1 + tall]) - own_rows(
+                    window[PAD - 1:PAD - 1 + tall])
                 across = across_held[k, pl.ds(local, high), pl.ds(local_col, width)]
-                downward = down_held[k, pl.ds(local, high), pl.ds(local_col, width)]
                 facing = (0.48 * across + 0.6 * downward + 1.28) * lax.rsqrt(
                     across * across + downward * downward + 4.0)
                 shading = 0.25 + 0.75 * jnp.maximum(facing, 0.0)
@@ -391,7 +388,7 @@
             pltpu.VMEM((rows, cols), ray_length.dtype),
             pltpu.SemaphoreType.DMA((rows // 16,)),
             pltpu.SemaphoreType.DMA,
-            *[pltpu.VMEM((slices, rows // groups, cols // subs), jnp.float32)] * 2,
+            pltpu.VMEM((slices, rows // groups, cols // subs), jnp.float32),
             pltpu.VMEM((chunks, 5, members // 2, 2, block, LANES), jnp.float32),
             pltpu.VMEM((chunks, 5, half, block, LANES), jnp.float32),
             *[pltpu.VMEM((chunks, half, block, LANES), jnp.float32)] * (bits - 1),

time: 69.2 us -> 62.6 us (0.905)
  Pallas kernels: 66.1 us -> 59.5 us
    pallas_call x1, Pallas kernels: 66.1 us -> 59.5 us  [body(): pl.pallas_call(functools.partial(kernel, cfg), out_shape=jax.ShapeDtypeSt...]
where the time goes in v3:
time: 62.6 us; the launch traced here: 62.4 us
  Pallas kernels  59.5 us (95%)
  local copies, waits for them, and re-layouts  1.67 us (3%)
  between operations  1.3 us (2%)
    pallas_call x1, Pallas kernels, body(): pl.pallas_call(functools.partial(kernel, cfg), out_shape=jax.ShapeDtypeSt...  59.5 us
    unnamed x1, local copies, waits for them, and re-layouts  1.67 us

profile of v3, /device:TPU:0, one launch (start us, length us, event | category | flops | bytes accessed | tf_op | source)
XLA Modules:
  0.0 62.4 jit_solution(1731649856805485580)
XLA Ops:
  1.3 59.5 %shard_map.46 = f32[5,8192]{1,0:T(8,128)} custom-call(bf16[8,128,2048]{2,1,0:T(8,128)(2,1)} %level_ref.1, s32[128,2048]{1,0:T(8,128)} %ray_ref.1, s32[1]{0:T(128)S(6)} %copy.6.mflip_ref, s32[1]{0:T(128)S(6)} %copy.7.gflip_ref), custom_call_target="tpu_custom_call" | custom-call | flops 83886080 | bytes 4194304 | tf_op jit(solution)/shard_map/pallas_call | solution.py:381
  60.8 1.7 %copy.8 = f32[5,8192]{1,0:T(8,128)} copy(f32[5,8192]{1,0:T(8,128)} %shard_map.46) | data formatting | bytes 327680

commit v4 on v0

--- a/solution.py
+++ b/solution.py
@@ -225,6 +225,11 @@
     def _(t):
         hand_over(t).wait_recv()
 
+    def put(c, s, value):
+        for q in range(block):
+            at = (q // tiles_wide) * cols + (q % tiles_wide) * LANES + s * chunk_cols
+            out_ref[c:c + 1, at:at + LANES] = value[q:q + 1, :]
+
     senders = [(group_id + 2 * groups - 1 - i) % groups for i in range(groups)]
     ranks = [jnp.bitwise_xor(s, group_mask) for s in senders]
     for s in range(subs):
@@ -247,8 +252,8 @@
                 term = ahead * piece(i, c)
                 total[c] = term if total[c] is None else total[c] + term
         for c in range(4):
-            out_ref[c, s] = total[c]
-        out_ref[4, s] = 1.0 - functools.reduce(lambda a, b: a * b, clear)
+            put(c, s, total[c])
+        put(4, s, 1.0 - functools.reduce(lambda a, b: a * b, clear))
 
     @pl.loop(0, chunks)
     def _(t):
@@ -279,9 +284,9 @@
     vmem = pl.BlockSpec(memory_space=pltpu.VMEM)
     anywhere = pl.BlockSpec(memory_space=pl.ANY)
     smem = pl.BlockSpec(memory_space=pltpu.SMEM)
-    image = pl.pallas_call(
+    return pl.pallas_call(
         functools.partial(kernel, cfg),
-        out_shape=jax.ShapeDtypeStruct((5, subs, block, LANES), jnp.float32),
+        out_shape=jax.ShapeDtypeStruct((5, pixels), jnp.float32),
         in_specs=[anywhere, anywhere, smem, smem],
         out_specs=vmem,
         scratch_shapes=[
@@ -304,9 +309,6 @@
             flops=40 * slices * rows * cols, bytes_accessed=level_set.size * 2,
             transcendentals=2 * slices * rows * cols),
     )(level_set, ray_length, member_flip, group_flip)
-    if subs > 1:
-        image = image.reshape(5, subs, pixels // cols, cols // subs).transpose(0, 2, 1, 3)
-    return image.reshape(5, pixels)
 
 
 def solution(mesh):

time: 58.1 us -> 58 us (level)
    reshape x2 -> x0, local copies, waits for them, and re-layouts: 1.79 us -> none  [the longest x1 0.97 us: body(): image.reshape(5, subs, pixels // cols, cols // subs).transpose(0, 2, 1, 3)]
    unnamed x0 -> x1, local copies, waits for them, and re-layouts: none -> 1.67 us
where the time goes in v4:
time: 58 us; the launch traced here: 57.9 us
  Pallas kernels  54.9 us (95%)
  local copies, waits for them, and re-layouts  1.67 us (3%)
  between operations  1.3 us (2%)
    pallas_call x1, Pallas kernels, body(): pl.pallas_call(functools.partial(kernel, cfg), out_shape=jax.ShapeDtypeSt...  54.9 us
    unnamed x1, local copies, waits for them, and re-layouts  1.67 us

profile of v4, /device:TPU:0, one launch (start us, length us, event | category | flops | bytes accessed | tf_op | source)
XLA Modules:
  0.0 57.9 jit_solution(15591695575053506626)
XLA Ops:
  1.3 54.9 %shard_map.46 = f32[5,8192]{1,0:T(8,128)} custom-call(bf16[8,128,2048]{2,1,0:T(8,128)(2,1)} %level_ref.1, s32[128,2048]{1,0:T(8,128)} %ray_ref.1, s32[1]{0:T(128)S(6)} %copy.6.mflip_ref, s32[1]{0:T(128)S(6)} %copy.7.gflip_ref), custom_call_target="tpu_custom_call" | custom-call | flops 83886080 | bytes 4194304 | tf_op jit(solution)/shard_map/pallas_call | solution.py:287
  56.2 1.7 %copy.8 = f32[5,8192]{1,0:T(8,128)} copy(f32[5,8192]{1,0:T(8,128)} %shard_map.46) | data formatting | bytes 327680
